TPU v7x, 512 devices: a whole 4x8x8 slice. The times are simulated.
512 devices in a mesh: section: 64 (over y_lo, z, core), uly: 8 (over x, y_hi).
Axes of the slice: x: 4, y: 8 (y_hi: 2, y_lo: 4; y = y_hi * 4 + y_lo), z: 8, core: 2. Of those that a mesh axis runs over, the one named last changes fastest.
Arguments:
- block_in: bfloat16 [64, 64, 2048], P('section', 'uly'), may hold values from -6 to 6
- fresh_patches: bfloat16 [3, 64, 2048], P(None, 'uly'), may hold values from -6 to 6
- w_qkv: bfloat16 [64, 2048, 3, 2048], P('section', None, None, 'uly'), may hold values from -0.125 to 0.125
- mod_shift: float32 [64, 2048], P('section'), may hold values from -3 to 3
- mod_scale: float32 [64, 2048], P('section'), may hold values from -0.5 to 0.5
- gate: float32 [64, 2048], P('section'), may hold values from 1 to 3
- q_gain: float32 [64, 128], P('section'), may hold values from 0.5 to 1.5
- k_gain: float32 [64, 128], P('section'), may hold values from 0.5 to 1.5
- image_cache: bfloat16 [64, 2, 512, 2048], P('section', None, None, 'uly'), may hold values from -6 to 6
- text_cache: bfloat16 [64, 2, 128, 2048], P('section', None, None, 'uly'), may hold values from -6 to 6
- patch_order: int32 [8], replicated, may hold values from 0 to 7, each once
- text_length: int32 [1], replicated, may hold values from 64 to 128
Outputs:
- block_out: bfloat16 [64, 64, 2048], P('section', 'uly')
- cache_out: bfloat16 [64, 2, 512, 2048], P('section', None, None, 'uly')
All inputs are finite; a program needn't handle non-finite values.
Results may differ from a plain program's by a relative error of at most 0.0095.
Values may be sent and summed in bfloat16 or wider, within the bound.
A program may use at most 64 MiB of HBM per device.

v0:
```python
import math

import jax
import jax.numpy as jnp
from jax import lax
from jax.sharding import PartitionSpec as P


def passed_along(value, axis, steps):
    count = lax.axis_size(axis)
    first, last = (max(0, -steps), min(count, count - steps))
    return lax.ppermute(value, axis, [(source, source + steps) for source in range(first, last)])


def head_norm(values, gain, heads):
    shaped = values.reshape(values.shape[0], heads, -1)
    factor = lax.rsqrt(jnp.mean(shaped * shaped, axis=-1, keepdims=True) + 1e-06)
    return (shaped * factor * gain).reshape(values.shape)


def modulate(stream, shift_row, scale_row):
    xf = stream.astype(jnp.float32)
    centered = xf - jnp.mean(xf, axis=-1, keepdims=True)
    variance = jnp.mean(centered * centered, axis=-1, keepdims=True)
    return (centered * lax.rsqrt(variance + 1e-06) * (1.0 + scale_row) + shift_row).astype(
        jnp.bfloat16
    )


def attend(queries, text_keys, text_values, image_keys, image_values, text_valid, heads):
    count = queries.shape[0]
    query_heads = queries.reshape(count, heads, -1)
    head_dim = query_heads.shape[-1]

    def exp_scores(keys):
        shaped = keys.reshape(keys.shape[0], heads, head_dim)
        raw = jnp.einsum("rhd,khd->hrk", query_heads, shaped, preferred_element_type=jnp.float32)
        return jnp.exp(raw / math.sqrt(head_dim))

    text_terms = exp_scores(text_keys) * text_valid
    image_terms = exp_scores(image_keys)
    total = jnp.sum(text_terms, axis=-1, keepdims=True) + jnp.sum(
        image_terms, axis=-1, keepdims=True
    )
    text_weights = (text_terms / total).astype(jnp.bfloat16)
    image_weights = (image_terms / total).astype(jnp.bfloat16)
    mixed = jnp.einsum(
        "hrk,khd->rhd",
        text_weights,
        text_values.reshape(-1, heads, head_dim),
        preferred_element_type=jnp.float32,
    )
    mixed = mixed + jnp.einsum(
        "hrk,khd->rhd",
        image_weights,
        image_values.reshape(-1, heads, head_dim),
        preferred_element_type=jnp.float32,
    )
    return mixed.astype(jnp.bfloat16).reshape(count, heads * head_dim)


def body(
    block_in,
    fresh_patches,
    w_qkv,
    mod_shift,
    mod_scale,
    gate,
    q_gain,
    k_gain,
    image_cache,
    text_cache,
    patch_order,
    text_length,
):
    section = lax.axis_index("section")
    rows_dev = block_in.shape[1]
    rows = rows_dev * lax.axis_size("uly")
    width = block_in.shape[2]
    local = w_qkv.shape[3]
    head_dim = q_gain.shape[1]
    heads = local // head_dim
    count = patch_order.shape[0]
    ticks = fresh_patches.shape[0] + 1
    weights = w_qkv[0].reshape(width, 3 * local)
    shift_row = mod_shift[0]
    scale_row = mod_scale[0]
    gate_row = gate[0]
    q_row = q_gain[0]
    k_row = k_gain[0]
    text_valid = (jnp.arange(text_cache.shape[2]) < text_length[0]).astype(jnp.float32)
    text_keys = head_norm(text_cache[0, 0].astype(jnp.float32), k_row, heads).astype(jnp.bfloat16)
    text_values = text_cache[0, 1]
    cache_raw = image_cache[0]
    cache_keys = head_norm(cache_raw[0].astype(jnp.float32), k_row, heads).astype(jnp.bfloat16)
    stream, arrivals = (
        lax.all_gather(block_in[0], "uly", axis=0, tiled=True),
        lax.all_gather(fresh_patches, "uly", axis=1, tiled=True),
    )
    result = stream
    for tick in range(ticks):
        slot = jnp.mod(tick - section, count)
        patch = jnp.sum(jnp.where(jnp.arange(count) == slot, patch_order, 0))
        start = patch * rows
        modulated = modulate(stream, shift_row, scale_row)
        projected = jnp.dot(modulated, weights, preferred_element_type=jnp.float32)
        queries = head_norm(projected[:, :local], q_row, heads).astype(jnp.bfloat16)
        new_keys = projected[:, local : 2 * local].astype(jnp.bfloat16)
        new_values = projected[:, 2 * local :].astype(jnp.bfloat16)
        cache_raw = lax.dynamic_update_slice(
            cache_raw, jnp.stack([new_keys, new_values]), (jnp.int32(0), start, jnp.int32(0))
        )
        normed_new = head_norm(new_keys.astype(jnp.float32), k_row, heads).astype(jnp.bfloat16)
        cache_keys = lax.dynamic_update_slice(cache_keys, normed_new, (start, jnp.int32(0)))
        attended = attend(
            queries, text_keys, text_values, cache_keys, cache_raw[1], text_valid, heads
        )
        joined = lax.all_gather(attended, "uly", axis=1, tiled=True)
        result = (stream.astype(jnp.float32) + gate_row * joined.astype(jnp.float32)).astype(
            jnp.bfloat16
        )
        if tick + 1 < ticks:
            passed = passed_along(result, "section", 1)
            stream = jnp.where(section == 0, arrivals[tick], passed)
    result = lax.dynamic_slice_in_dim(result, lax.axis_index("uly") * rows_dev, rows_dev, 0)
    return (result[None], cache_raw[None])


def solution(mesh):
    in_specs = (
        P("section", "uly", None),
        P(None, "uly", None),
        P("section", None, None, "uly"),
        P("section", None),
        P("section", None),
        P("section", None),
        P("section", None),
        P("section", None),
        P("section", None, None, "uly"),
        P("section", None, None, "uly"),
        P(),
        P(),
    )
    out_specs = (P("section", "uly", None), P("section", None, None, "uly"))
    return jax.shard_map(body, mesh=mesh, in_specs=in_specs, out_specs=out_specs, check_vma=False)
```

profile of v0, /device:TPU:296, one launch (start us, length us, event | category | flops | bytes accessed | tf_op | source)
XLA Modules:
  0.0 405.5 jit_solution(7483691183382160541)
XLA Ops:
  0.7 2.1 copy.200
  2.7 1.0 convert_multiply_fusion
  3.8 1.5 fusion.141
  6.8 45.5 %all-gather = bf16[1,64,2048]{2,1,0:T(8,128)(2,1)S(1)} all-gather(bf16[1,8,2048]{2,1,0:T(8,128)(2,1)} %param.12), channel_id=2, replica_groups=mesh['section'=64,'uly'=8] {'uly'}, dimensions={1}, use_global_device_ids=true | all-gather | bytes 294912 | tf_op jit(solution)/shard_map/all_gather | solution.py:97
  55.4 3.2 copy.184
  59.0 1.1 fusion.142
  61.5 1.5 mul.442
  63.0 1.6 reduce_sum.276
  65.3 1.5 mul.434
  66.9 1.7 fusion.46
  70.0 1.0 copy.201
  71.0 1.8 dynamic_update_slice.25
  72.8 1.7 slice.103
  74.4 0.9 mul.415
  78.2 1.6 copy.248
  79.9 0.9 fusion.106
  80.8 1.2 fusion.144
  82.0 1.0 multiply_convert_fusion
  83.3 1.2 convolution_bitcast_fusion.7
  84.5 1.1 fusion.23
  85.6 44.9 %all_gather.20 = bf16[64,2048]{1,0:T(8,128)(2,1)S(1)} all-gather(bf16[64,256]{1,0:T(8,128)(2,1)S(1)} %bitcast.336), channel_id=1, replica_groups=mesh['section'=64,'uly'=8] {'uly'}, dimensions={1}, use_global_device_ids=true | all-gather | bytes 294912 | tf_op jit(solution)/shard_map/all_gather | solution.py:118
  131.3 2.0 collective-permute-start
  133.9 56.1 %all_gather.18 = bf16[3,64,2048]{2,1,0:T(8,128)(2,1)S(1)} all-gather(bf16[3,8,2048]{2,1,0:T(8,128)(2,1)} %param.13), channel_id=1, replica_groups=mesh['section'=64,'uly'=8] {'uly'}, dimensions={1}, use_global_device_ids=true | all-gather | bytes 884736 | tf_op jit(solution)/shard_map/all_gather | solution.py:98
  190.0 0.9 copy-done.5
  190.9 1.1 convert_reduce_fusion.1
  192.8 1.8 fusion.145
  195.8 0.9 mul.462
  200.0 1.7 dynamic_update_slice.27
  201.7 1.7 slice.107
  203.3 1.5 slice_multiply_fusion.2
  204.8 0.9 mul.455
  207.3 0.9 fusion.107
  208.2 0.8 fusion.146
  209.4 1.2 convolution_bitcast_fusion.6
  210.5 1.1 fusion.22
  211.6 45.4 %all_gather.21 = bf16[64,2048]{1,0:T(8,128)(2,1)S(1)} all-gather(bf16[64,256]{1,0:T(8,128)(2,1)S(1)} %bitcast.337), channel_id=1, replica_groups=mesh['section'=64,'uly'=8] {'uly'}, dimensions={1}, use_global_device_ids=true | all-gather | bytes 294912 | tf_op jit(solution)/shard_map/all_gather | solution.py:118
  257.1 1.7 fusion.48
  258.8 1.9 collective-permute-start.1
  261.4 6.6 %collective-permute-done.1 = bf16[64,2048]{1,0:T(8,128)(2,1)} collective-permute-done((bf16[64,2048]{1,0:T(8,128)(2,1)}, bf16[64,2048]{1,0:T(8,128)(2,1)}, u32[]{:S(2)}, u32[]{:S(2)}) %collective-permute-start.1) | collective-permute-done | bytes 262176 | tf_op jit(solution)/shard_map/ppermute | solution.py:12
  268.0 1.2 convert_reduce_fusion
  269.9 1.8 fusion.148
  273.0 0.9 mul.481
  277.1 2.4 dynamic_update_slice.29
  279.4 1.7 slice.111
  281.1 1.5 slice_multiply_fusion.1
  282.6 0.9 mul.474
  285.1 0.9 fusion.108
  286.0 0.8 fusion.149
  287.2 1.2 convolution_bitcast_fusion.5
  288.3 1.1 fusion.21
  289.4 45.0 %all_gather.22 = bf16[64,2048]{1,0:T(8,128)(2,1)S(1)} all-gather(bf16[64,256]{1,0:T(8,128)(2,1)S(1)} %bitcast.338), channel_id=1, replica_groups=mesh['section'=64,'uly'=8] {'uly'}, dimensions={1}, use_global_device_ids=true | all-gather | bytes 294912 | tf_op jit(solution)/shard_map/all_gather | solution.py:118
  334.4 1.7 fusion.49
  336.1 2.1 collective-permute-start.2
  338.9 6.4 %collective-permute-done.2 = bf16[64,2048]{1,0:T(8,128)(2,1)} collective-permute-done((bf16[64,2048]{1,0:T(8,128)(2,1)}, bf16[64,2048]{1,0:T(8,128)(2,1)}, u32[]{:S(2)}, u32[]{:S(2)}) %collective-permute-start.2) | collective-permute-done | bytes 262176 | tf_op jit(solution)/shard_map/ppermute | solution.py:12
  345.3 1.2 convert_reduce_fusion.3
  346.5 0.8 convert_element_type.212
  347.7 1.8 fusion.151
  351.4 2.3 dynamic_update_slice.31
  353.7 1.0 slice.115
  354.7 0.8 slice_multiply_fusion
  355.9 0.9 fusion.109
  357.8 45.1 %all_gather.23 = bf16[64,2048]{1,0:T(8,128)(2,1)S(1)} all-gather(bf16[64,256]{1,0:T(8,128)(2,1)S(1)} %bitcast.339), channel_id=1, replica_groups=mesh['section'=64,'uly'=8] {'uly'}, dimensions={1}, use_global_device_ids=true | all-gather | bytes 294912 | tf_op jit(solution)/shard_map/all_gather | solution.py:118
  403.0 1.0 copy.237
  404.0 1.5 fusion.105
  (129 shorter events, 28.9 us)
Async XLA Ops:
  0.6 76.2 %copy-start = (f32[1,128]{1,0:T(1,128)S(1)}, f32[1,128]{1,0:T(1,128)}, u32[]{:S(2)}) copy-start(f32[1,128]{1,0:T(1,128)} %param.18) | copy-start | bytes 1540
  0.6 53.3 %copy-start.22 = (f32[1,128]{1,0:T(1,128)S(1)}, f32[1,128]{1,0:T(1,128)}, u32[]{:S(2)}) copy-start(f32[1,128]{1,0:T(1,128)} %param.19) | copy-start | bytes 1540
  0.7 53.3 %copy-start.23 = (s32[8]{0:T(128)S(1)}, s32[8]{0:T(128)}, u32[]{:S(2)}) copy-start(s32[8]{0:T(128)} %param.22) | copy-start | bytes 100
  55.4 3.2 copy-start.21
  55.4 3.7 copy-start.10
  60.1 0.7 copy-start.6
  72.8 57.7 %copy-start.14 = (f32[1,2048]{1,0:T(1,128)S(1)}, f32[1,2048]{1,0:T(1,128)}, u32[]{:S(2)}) copy-start(f32[1,2048]{1,0:T(1,128)} %param.17) | copy-start | bytes 24580
  74.4 118.3 %copy-start.11 = (f32[1,2048]{1,0:T(1,128)S(1)}, f32[1,2048]{1,0:T(1,128)}, u32[]{:S(2)}) copy-start(f32[1,2048]{1,0:T(1,128)} %param.15) | copy-start | bytes 24580
  76.9 117.7 %copy-start.17 = (f32[256]{0:T(256)}, f32[256]{0:T(256)S(1)}, u32[]{:S(2)}) copy-start(f32[256]{0:T(256)S(1)} %broadcast_bitcast_fusion.1) | copy-start | bytes 3076
  77.5 117.0 %copy-start.19 = (f32[128]{0:T(128)}, f32[128]{0:T(128)S(1)}, u32[]{:S(2)}) copy-start(f32[128]{0:T(128)S(1)} %compare_convert_fusion) | copy-start | bytes 1540
  131.3 67.1 %copy-start.2 = (bf16[512,256]{1,0:T(8,128)(2,1)S(1)}, bf16[512,256]{1,0:T(8,128)(2,1)}, u32[]{:S(2)}) copy-start(bf16[512,256]{1,0:T(8,128)(2,1)} %get-tuple-element.33) | copy-start | bytes 786436
  131.3 58.8 %collective-permute-start = (bf16[64,2048]{1,0:T(8,128)(2,1)}, bf16[64,2048]{1,0:T(8,128)(2,1)}, u32[]{:S(2)}, u32[]{:S(2)}) collective-permute-start(bf16[64,2048]{1,0:T(8,128)(2,1)} %fusion.47), channel_id=1, source_target_pairs={{0,8},{8,16},{16,24},{24,32},{32,40},{40,48},{48,56},{56,64},{64,7... | collective-permute-start | bytes 786440 | tf_op jit(solution)/shard_map/ppermute | solution.py:12
  190.0 0.9 copy-start.5
  192.1 0.7 copy-start.3
  194.6 0.6 copy-start.8
  206.4 63.5 %copy-start.12 = (f32[1,2048]{1,0:T(1,128)S(1)}, f32[1,2048]{1,0:T(1,128)}, u32[]{:S(2)}) copy-start(f32[1,2048]{1,0:T(1,128)} %param.15) | copy-start | bytes 24580
  258.8 9.2 %collective-permute-start.1 = (bf16[64,2048]{1,0:T(8,128)(2,1)}, bf16[64,2048]{1,0:T(8,128)(2,1)}, u32[]{:S(2)}, u32[]{:S(2)}) collective-permute-start(bf16[64,2048]{1,0:T(8,128)(2,1)} %fusion.48), channel_id=1, source_target_pairs={{0,8},{8,16},{16,24},{24,32},{32,40},{40,48},{48,56},{56,64},{64,7... | collective-permute-start | bytes 786440 | tf_op jit(solution)/shard_map/ppermute | solution.py:12
  269.2 0.7 copy-start.4
  271.7 0.6 copy-start.9
  284.2 63.4 %copy-start.13 = (f32[1,2048]{1,0:T(1,128)S(1)}, f32[1,2048]{1,0:T(1,128)}, u32[]{:S(2)}) copy-start(f32[1,2048]{1,0:T(1,128)} %param.15) | copy-start | bytes 24580
  336.1 9.2 %collective-permute-start.2 = (bf16[64,2048]{1,0:T(8,128)(2,1)}, bf16[64,2048]{1,0:T(8,128)(2,1)}, u32[]{:S(2)}, u32[]{:S(2)}) collective-permute-start(bf16[64,2048]{1,0:T(8,128)(2,1)} %fusion.49), channel_id=1, source_target_pairs={{0,8},{8,16},{16,24},{24,32},{32,40},{40,48},{48,56},{56,64},{64,7... | collective-permute-start | bytes 786440 | tf_op jit(solution)/shard_map/ppermute | solution.py:12
  347.4 8.5 %copy-start.18 = (f32[256]{0:T(256)S(1)}, f32[256]{0:T(256)}, u32[]{:S(2)}) copy-start(f32[256]{0:T(256)} %copy-done.17) | copy-start | bytes 3076
  347.6 9.1 %copy-start.20 = (f32[128]{0:T(128)S(1)}, f32[128]{0:T(128)}, u32[]{:S(2)}) copy-start(f32[128]{0:T(128)} %copy-done.19) | copy-start | bytes 1540
  349.4 0.6 copy-start.7
  349.4 8.2 %copy-start.16 = (bf16[1,1,128,256]{2,3,1,0:T(8,128)(2,1)S(1)}, bf16[1,1,128,256]{2,3,1,0:T(8,128)(2,1)}, u32[]{:S(2)}) copy-start(bf16[1,1,128,256]{2,3,1,0:T(8,128)(2,1)} %copy.248) | copy-start | bytes 196612
  349.4 54.6 %copy-start.15 = (f32[1,2048]{1,0:T(1,128)S(1)}, f32[1,2048]{1,0:T(1,128)}, u32[]{:S(2)}) copy-start(f32[1,2048]{1,0:T(1,128)} %param.17) | copy-start | bytes 24580
  353.7 49.3 %copy-start.1 = (bf16[2,512,256]{1,2,0:T(8,128)(2,1)S(1)}, bf16[2,512,256]{1,2,0:T(8,128)(2,1)}, u32[]{:S(2)}) copy-start(bf16[2,512,256]{1,2,0:T(8,128)(2,1)} %dynamic_update_slice.31) | copy-start | bytes 1572868
where the time goes:
time: 408 us; the launch traced here: 405 us
  blocking collectives  282 us (69%)
  other arithmetic  41.5 us (10%)
  local copies, waits for them, and re-layouts  40.3 us (10%)
  matrix products  17.9 us (4%)
  waiting for transfers between devices  13 us (3%)
  starting transfers between devices  6.04 us (1%)
  between operations  4.57 us (1%)
    all_gather x4, blocking collectives, body(): joined = lax.all_gather(attended, 'uly', axis=1, tiled=True)  180 us
    all_gather x1, blocking collectives, body(): lax.all_gather(fresh_patches, 'uly', axis=1, tiled=True)  56.1 us
    all_gather x1, blocking collectives, body(): lax.all_gather(block_in[0], 'uly', axis=0, tiled=True)  45.5 us
    ppermute x3, waiting for transfers between devices, passed_along(): lax.ppermute(value, axis, [(source, source + steps) for source in range(f...  13 us
    unnamed x53, local copies, waits for them, and re-layouts  12.4 us
    dynamic_update_slice x4, local copies, waits for them, and re-layouts, body(): lax.dynamic_update_slice(cache_raw, jnp.stack([new_keys, new_values]), (j...  8.19 us
  transfers between devices with their start and end apart: 3, of which 2 were waited for; matrix products, arithmetic and copies ran while one was open for 0% of the time, Pallas kernels for 0%

commit v1 on v0

v1 whole, which is shorter than its diff:
```python
import functools
import math

import jax
import jax.numpy as jnp
from jax import lax
from jax.experimental import pallas as pl
from jax.experimental.pallas import tpu as pltpu
from jax.sharding import PartitionSpec as P

MESH = pl.DeviceIdType.MESH
F32 = jnp.float32
BF16 = jnp.bfloat16
EPS = 1e-06


def head_factor(values):
    return lax.rsqrt(jnp.mean(values * values, axis=-1, keepdims=True) + EPS)


def normed(values, gain, head_dim):
    parts = []
    for start in range(0, values.shape[1], head_dim):
        part = values[:, start : start + head_dim]
        parts.append(part * head_factor(part) * gain)
    return jnp.concatenate(parts, axis=1)


def kernel(
    dims,
    block_hbm,
    fresh_hbm,
    w_hbm,
    shift_hbm,
    scale_hbm,
    gate_hbm,
    q_gain_hbm,
    k_gain_hbm,
    image_hbm,
    text_hbm,
    order_ref,
    length_ref,
    out_ref,
    cache_out_hbm,
    block,
    fresh,
    w,
    shift,
    scale,
    gate,
    q_gain,
    k_gain,
    raw,
    text,
    keys,
    values,
    stream,
    mod,
    sent,
    row_send,
    row_recv,
    last_send,
    last_recv,
    cache_stage,
    load_sem,
    store_sem,
    row_send_sem,
    row_recv_sem,
    tick_send_sem,
    tick_recv_sem,
    last_send_sem,
    last_recv_sem,
):
    sections, group, ticks, patches, pr, width, local, hd, txt = dims
    heads = local // hd
    img = patches * pr
    rows_dev = pr // group
    half = width // 2
    section = lax.axis_index("section")
    uly = lax.axis_index("uly")

    def peer(k):
        return lax.rem(uly + k, group)

    barrier = pltpu.get_barrier_semaphore()
    for k in range(1, group):
        pl.semaphore_signal(barrier, inc=1, device_id=(section, peer(k)), device_id_type=MESH)

    @pl.when(section > 0)
    def _():
        for k in range(group):
            pl.semaphore_signal(barrier, inc=1, device_id=(section - 1, peer(k)), device_id_type=MESH)

    loads = [
        pltpu.make_async_copy(src, dst, load_sem.at[i])
        for i, (src, dst) in enumerate(
            [
                (block_hbm, block),
                (fresh_hbm, fresh),
                (text_hbm, text),
                (k_gain_hbm, k_gain),
                (image_hbm, raw.at[:, pl.ds(0, img), :]),
                (shift_hbm, shift),
                (scale_hbm, scale),
                (gate_hbm, gate),
                (q_gain_hbm, q_gain),
                (w_hbm, w),
            ]
        )
    ]
    for copy in loads:
        copy.start()

    loads[0].wait()
    loads[1].wait()
    own = block[...].astype(F32)
    row_send[0] = jnp.concatenate([own[:, :half], own[:, half:]], axis=0).astype(BF16)
    for t in range(1, ticks):
        own = fresh[t - 1].astype(F32)
        row_send[t] = jnp.concatenate([own[:, :half], own[:, half:]], axis=0).astype(BF16)

    pl.semaphore_wait(barrier, group - 1 + jnp.where(section < sections - 1, group, 0))

    def row_copy(t, k):
        return pltpu.make_async_remote_copy(
            src_ref=row_send.at[t],
            dst_ref=row_recv.at[t, uly],
            send_sem=row_send_sem.at[t, k],
            recv_sem=row_recv_sem.at[t, uly],
            device_id=(section, peer(k)),
            device_id_type=MESH,
        )

    def row_arrival(t, k):
        return pltpu.make_async_remote_copy(
            src_ref=row_send.at[t],
            dst_ref=row_recv.at[t, peer(k)],
            send_sem=row_send_sem.at[t, k],
            recv_sem=row_recv_sem.at[t, peer(k)],
            device_id=(section, peer(k)),
            device_id_type=MESH,
        )

    for k in range(1, group):
        row_copy(0, k).start()

    @pl.when(section == 0)
    def _():
        for t in range(1, ticks):
            for k in range(1, group):
                row_copy(t, k).start()

    row_recv[0, uly] = row_send[0]
    for t in range(1, ticks):
        row_recv[t, uly] = row_send[t]

    def patch_at(slot):
        return order_ref[lax.rem(slot - section + sections * patches, patches)]

    loads[2].wait()
    loads[3].wait()
    loads[4].wait()
    k_row = k_gain[...]
    keys[pl.ds(0, txt), :] = normed(text[0].astype(F32), k_row, hd).astype(BF16)
    values[pl.ds(0, txt), :] = text[1]
    for j in range(patches):
        patch = patch_at(j)
        met = []
        for i in range(2):
            rows = raw[i, pl.ds(0, pr), :]
            for b in range(1, patches):
                rows = jnp.where(patch == b, raw[i, pl.ds(b * pr, pr), :], rows)
            met.append(rows)
        keys[pl.ds(txt + j * pr, pr), :] = normed(met[0].astype(F32), k_row, hd).astype(BF16)
        values[pl.ds(txt + j * pr, pr), :] = met[1]
    for copy in loads[5:]:
        copy.wait()
    q_row = q_gain[...]
    valid = (
        lax.broadcasted_iota(jnp.int32, (1, txt), 1) < length_ref[0]
    ).astype(F32)

    def rows_to_stream(t):
        for k in range(1, group):
            row_arrival(t, k).wait_recv()
        pieces = [row_recv[t, i].astype(F32) for i in range(group)]
        for side in range(2):
            whole = jnp.concatenate(
                [piece[side * rows_dev : (side + 1) * rows_dev] for piece in pieces], axis=0
            ).astype(BF16)
            for c in range(group // 2):
                stream[t, side * (group // 2) + c] = whole[:, c * local : (c + 1) * local]

    def tick_copy(t, k):
        return pltpu.make_async_remote_copy(
            src_ref=sent.at[t],
            dst_ref=stream.at[t + 1, uly],
            send_sem=tick_send_sem.at[t, k],
            recv_sem=tick_recv_sem.at[t + 1, uly],
            device_id=(section + 1, peer(k)),
            device_id_type=MESH,
        )

    def tick_arrival(t, k):
        return pltpu.make_async_remote_copy(
            src_ref=sent.at[t],
            dst_ref=stream.at[t, k],
            send_sem=tick_send_sem.at[t, k],
            recv_sem=tick_recv_sem.at[t, k],
            device_id=(section, uly),
            device_id_type=MESH,
        )

    def last_copy(k):
        return pltpu.make_async_remote_copy(
            src_ref=last_send.at[peer(k)],
            dst_ref=last_recv.at[uly],
            send_sem=last_send_sem.at[k],
            recv_sem=last_recv_sem.at[uly],
            device_id=(section, peer(k)),
            device_id_type=MESH,
        )

    def last_arrival(k):
        return pltpu.make_async_remote_copy(
            src_ref=last_send.at[peer(k)],
            dst_ref=last_recv.at[peer(k)],
            send_sem=last_send_sem.at[k],
            recv_sem=last_recv_sem.at[peer(k)],
            device_id=(section, peer(k)),
            device_id_type=MESH,
        )

    for t in range(ticks):
        if t == 0:
            rows_to_stream(0)
        else:

            @pl.when(section == 0)
            def _():
                rows_to_stream(t)

            @pl.when(section > 0)
            def _():
                for k in range(group):
                    tick_arrival(t, k).wait_recv()

        chunks = [stream[t, c].astype(F32) for c in range(group)]
        mean = jnp.sum(sum(chunks), axis=-1, keepdims=True) / width
        centered = [chunk - mean for chunk in chunks]
        variance = jnp.sum(sum(c * c for c in centered), axis=-1, keepdims=True) / width
        factor = lax.rsqrt(variance + EPS)
        for c in range(group):
            at = pl.ds(c * local, local)
            mod[:, at] = (centered[c] * factor * (1.0 + scale[:, at]) + shift[:, at]).astype(BF16)
        queries, new_keys, new_values = [
            jnp.dot(mod[...], w[j], preferred_element_type=F32) for j in range(3)
        ]
        queries = normed(queries, q_row, hd).astype(BF16)
        new_keys = new_keys.astype(BF16)
        new_values = new_values.astype(BF16)
        raw[0, pl.ds(img + t * pr, pr), :] = new_keys
        raw[1, pl.ds(img + t * pr, pr), :] = new_values
        keys[pl.ds(txt + t * pr, pr), :] = normed(new_keys.astype(F32), k_row, hd).astype(BF16)
        values[pl.ds(txt + t * pr, pr), :] = new_values

        if t == ticks - 1:
            for b in range(patches):
                for i in range(2):
                    rows = raw[i, pl.ds(b * pr, pr), :]
                    for j in range(ticks):
                        rows = jnp.where(
                            patch_at(j) == b, raw[i, pl.ds(img + j * pr, pr), :], rows
                        )
                    cache_stage[i, pl.ds(b * pr, pr), :] = rows
            store = pltpu.make_async_copy(cache_stage, cache_out_hbm, store_sem)
            store.start()

        results = []
        for h in range(heads):
            at = slice(h * hd, (h + 1) * hd)
            score = lax.dot_general(
                queries[:, at],
                keys[:, at],
                (((1,), (1,)), ((), ())),
                preferred_element_type=F32,
            )
            term = jnp.exp(score * (1.0 / math.sqrt(hd)))
            term = jnp.concatenate([term[:, :txt] * valid, term[:, txt:]], axis=1)
            total = jnp.sum(term, axis=-1, keepdims=True)
            weight = (term / total).astype(BF16)
            results.append(jnp.dot(weight, values[:, at], preferred_element_type=F32))
        attended = jnp.concatenate(results, axis=1).astype(BF16).astype(F32)
        own_at = pl.ds(pl.multiple_of(uly * local, local), local)
        result = stream[t, uly].astype(F32) + gate[:, own_at] * attended

        if t < ticks - 1:
            sent[t] = result.astype(BF16)

            @pl.when(section < sections - 1)
            def _():
                for k in range(group):
                    tick_copy(t, k).start()
        else:
            for i in range(group):
                piece = result[i * rows_dev : (i + 1) * rows_dev]
                last_send[i] = jnp.concatenate(
                    [piece[:, c * hd : (c + 1) * hd] for c in range(heads)], axis=0
                ).astype(BF16)
            for k in range(1, group):
                last_copy(k).start()
            last_recv[uly] = last_send[uly]

    for k in range(1, group):
        row_copy(0, k).wait_send()

    @pl.when(section == 0)
    def _():
        for t in range(1, ticks):
            for k in range(1, group):
                row_copy(t, k).wait_send()

    @pl.when(section < sections - 1)
    def _():
        for t in range(ticks - 1):
            for k in range(group):
                tick_copy(t, k).wait_send()

    for k in range(1, group):
        last_arrival(k).wait_recv()
    for i in range(group):
        piece = last_recv[i].astype(F32)
        for c in range(heads):
            out_ref[:, pl.ds(i * local + c * hd, hd)] = piece[
                c * rows_dev : (c + 1) * rows_dev
            ].astype(BF16)
    for k in range(1, group):
        last_copy(k).wait_send()
    store.wait()


def body(
    block_in,
    fresh_patches,
    w_qkv,
    mod_shift,
    mod_scale,
    gate,
    q_gain,
    k_gain,
    image_cache,
    text_cache,
    patch_order,
    text_length,
):
    sections, group = lax.axis_size("section"), lax.axis_size("uly")
    rows_dev, width = block_in.shape[1:]
    local = w_qkv.shape[3]
    hd = q_gain.shape[1]
    patches = patch_order.shape[0]
    ticks = fresh_patches.shape[0] + 1
    pr = rows_dev * group
    txt = text_cache.shape[2]
    img = patches * pr
    heads = local // hd
    dims = (sections, group, ticks, patches, pr, width, local, hd, txt)
    hbm = pl.BlockSpec(memory_space=pltpu.HBM)
    smem = pl.BlockSpec(memory_space=pltpu.SMEM)
    dma = pltpu.SemaphoreType.DMA
    out, cache = pl.pallas_call(
        functools.partial(kernel, dims),
        out_shape=(
            jax.ShapeDtypeStruct((rows_dev, width), BF16),
            jax.ShapeDtypeStruct((2, img, local), BF16),
        ),
        in_specs=[hbm] * 10 + [smem] * 2,
        out_specs=(pl.BlockSpec(memory_space=pltpu.VMEM), hbm),
        scratch_shapes=[
            pltpu.VMEM((rows_dev, width), BF16),
            pltpu.VMEM((ticks - 1, rows_dev, width), BF16),
            pltpu.VMEM((3, width, local), BF16),
            pltpu.VMEM((1, width), F32),
            pltpu.VMEM((1, width), F32),
            pltpu.VMEM((1, width), F32),
            pltpu.VMEM((1, hd), F32),
            pltpu.VMEM((1, hd), F32),
            pltpu.VMEM((2, img + ticks * pr, local), BF16),
            pltpu.VMEM((2, txt, local), BF16),
            pltpu.VMEM((txt + img, local), BF16),
            pltpu.VMEM((txt + img, local), BF16),
            pltpu.VMEM((ticks, group, pr, local), BF16),
            pltpu.VMEM((pr, width), BF16),
            pltpu.VMEM((ticks, pr, local), BF16),
            pltpu.VMEM((ticks, 2 * rows_dev, width // 2), BF16),
            pltpu.VMEM((ticks, group, 2 * rows_dev, width // 2), BF16),
            pltpu.VMEM((group, heads * rows_dev, hd), BF16),
            pltpu.VMEM((group, heads * rows_dev, hd), BF16),
            pltpu.VMEM((2, img, local), BF16),
            dma((10,)),
            dma,
            dma((ticks, group)),
            dma((ticks, group)),
            dma((ticks, group)),
            dma((ticks, group)),
            dma((group,)),
            dma((group,)),
        ],
        compiler_params=pltpu.CompilerParams(
            collective_id=0, has_side_effects=True, vmem_limit_bytes=63 * 1024 * 1024
        ),
    )(
        block_in[0],
        fresh_patches,
        jnp.transpose(w_qkv[0], (1, 0, 2)),
        mod_shift,
        mod_scale,
        gate,
        q_gain,
        k_gain,
        image_cache[0],
        text_cache[0],
        patch_order,
        text_length,
    )
    return out[None], cache[None]


def solution(mesh):
    in_specs = (
        P("section", "uly", None),
        P(None, "uly", None),
        P("section", None, None, "uly"),
        P("section", None),
        P("section", None),
        P("section", None),
        P("section", None),
        P("section", None),
        P("section", None, None, "uly"),
        P("section", None, None, "uly"),
        P(),
        P(),
    )
    out_specs = (P("section", "uly", None), P("section", None, None, "uly"))
    return jax.shard_map(body, mesh=mesh, in_specs=in_specs, out_specs=out_specs, check_vma=False)
```

time: 408 us -> 70.7 us (0.17)
  the two profiles are of different devices: /device:TPU:296 before, /device:TPU:16 now
where the time goes in v1:
time: 70.7 us; the launch traced here: 70.4 us
  Pallas kernels  65.9 us (93%)
  local copies, waits for them, and re-layouts  3.24 us (5%)
  between operations  1.29 us (2%)
    pallas_call x1, Pallas kernels, body(): pl.pallas_call(functools.partial(kernel, dims), out_shape=(jax.ShapeDtype...  65.9 us
    unnamed x2, local copies, waits for them, and re-layouts  3.24 us

profile of v1, /device:TPU:16, one launch (start us, length us, event | category | flops | bytes accessed | tf_op | source)
XLA Modules:
  0.0 70.4 jit_solution(11195203383567164948)
XLA Ops:
  1.3 65.9 %shard_map.131 = (bf16[8,2048]{1,0:T(8,128)(2,1)}, bf16[2,512,256]{2,1,0:T(8,128)(2,1)}) custom-call(bf16[8,2048]{1,0:T(8,128)(2,1)} %bitcast.12, bf16[3,8,2048]{2,1,0:T(8,128)(2,1)} %fresh_hbm.1, bf16[3,2048,256]{2,1,0:T(8,128)(2,1)} %bitcast.8, f32[1,2048]{1,0:T(1,128)} %shift_hbm.1, f32[1,2048]{1,0:T(1,128)} %scale_hbm.1, f32[1,2048]{1,0:T(1,128)} %gate_hbm.1, ...), custom_call_target="tpu_custom_call" | custom-call | tf_op jit(solution)/shard_map/pallas_call | solution.py:370
  67.2 1.4 %copy.17 = bf16[1,8,2048]{2,1,0:T(8,128)(2,1)} copy(bf16[1,8,2048]{2,1,0:T(8,128)(2,1)} %bitcast.13) | data formatting | bytes 65536
  68.6 1.9 %copy.18 = bf16[1,2,512,256]{3,2,1,0:T(8,128)(2,1)} copy(bf16[1,2,512,256]{3,2,1,0:T(8,128)(2,1)} %bitcast.10) | data formatting | bytes 1048576

commit v2 on v1

v2 whole, which is shorter than its diff:
```python
import functools
import math

import jax
import jax.numpy as jnp
from jax import lax
from jax.experimental import pallas as pl
from jax.experimental.pallas import tpu as pltpu
from jax.sharding import PartitionSpec as P

MESH = pl.DeviceIdType.MESH
F32 = jnp.float32
BF16 = jnp.bfloat16
EPS = 1e-06
VMEM_LIMIT = 63 * 1024 * 1024


def head_factor(values):
    return lax.rsqrt(jnp.mean(values * values, axis=-1, keepdims=True) + EPS)


def normed(values, gain, head_dim):
    parts = []
    for start in range(0, values.shape[1], head_dim):
        part = values[:, start : start + head_dim]
        parts.append(part * head_factor(part) * gain)
    return jnp.concatenate(parts, axis=1)


def fold(w, shift, scale, plain_sum, shift_sum, local):
    width = w.shape[1]
    block = 256
    first = lax.broadcasted_iota(jnp.int32, (16, block), 0)
    ones = jnp.ones((16, block), BF16)

    def step(i, totals):
        at = pl.ds(pl.multiple_of(i * block, block), block)
        shift_row = shift[:, at]
        high = shift_row.astype(BF16).astype(F32)
        both = jnp.where(first == 0, high, jnp.where(first == 1, shift_row - high, 0.0))
        both = both.astype(BF16)
        factors = []
        for part in range(block // 128):
            row = scale[:, pl.ds(pl.multiple_of(i * block + part * 128, 128), 128)]
            factors.append(jnp.transpose(jnp.broadcast_to(1.0 + row, (128, 128))))
        factor = jnp.concatenate(factors, axis=0)
        new = []
        for j in range(3):
            rows = w[j, at, :]
            folded = jnp.concatenate(
                [
                    (rows[:, c : c + 128].astype(F32) * factor).astype(BF16)
                    for c in range(0, local, 128)
                ],
                axis=1,
            )
            w[j, at, :] = folded
            new.append(totals[2 * j] + jnp.dot(ones, folded, preferred_element_type=F32))
            new.append(totals[2 * j + 1] + jnp.dot(both, rows, preferred_element_type=F32))
        return tuple(new)

    zero = jnp.zeros((16, local), F32)
    totals = lax.fori_loop(0, width // block, step, (zero,) * 6)
    for j in range(3):
        plain_sum[j] = totals[2 * j][:1]
        shift_sum[j] = totals[2 * j + 1][:1] + totals[2 * j + 1][1:2]


def lanes_summed(values):
    return sum(values[:, c : c + 128] for c in range(0, values.shape[1], 128))


def project(stream, order, arrived, w, plain_sum, shift_sum, local, width):
    near = len(order) // 2
    sums = [None] * 3

    def add(chunk, c):
        at = pl.ds(pl.multiple_of(c * local, local), local)
        for j in range(3):
            product = jnp.dot(chunk, w[j, at, :], preferred_element_type=F32)
            sums[j] = product if sums[j] is None else sums[j] + product

    values = []
    for c in order[:near]:
        arrived(c)
        chunk = stream[c]
        add(chunk, c)
        values.append(chunk.astype(F32))
    pivot = jnp.sum(lanes_summed(sum(values)), axis=-1, keepdims=True) / (near * local)
    off = [value - pivot for value in values]
    first = lanes_summed(sum(off))
    second = lanes_summed(sum(o * o for o in off))
    for c in order[near:]:
        arrived(c)
        chunk = stream[c]
        add(chunk, c)
        o = chunk.astype(F32) - pivot
        first = first + lanes_summed(o)
        second = second + lanes_summed(o * o)
    beyond = jnp.sum(first, axis=-1, keepdims=True) / width
    variance = jnp.sum(second, axis=-1, keepdims=True) / width - beyond * beyond
    factor = lax.rsqrt(variance + EPS)
    mean = pivot + beyond
    return [factor * (sums[j] - mean * plain_sum[j]) + shift_sum[j] for j in range(3)]


def attend(queries, q_row, keys_kept, values_kept, keys_met, values_met, valid, hd):
    txt = valid.shape[1]
    results = []
    for start in range(0, queries.shape[1], hd):
        at = slice(start, start + hd)
        query = queries[:, at]
        factor = head_factor(query) * (1.0 / math.sqrt(hd))
        query = (query * q_row).astype(BF16)
        contract = (((1,), (1,)), ((), ()))
        kept = lax.dot_general(query, keys_kept[:, at], contract, preferred_element_type=F32)
        met = lax.dot_general(query, keys_met[:, at], contract, preferred_element_type=F32)
        kept = jnp.exp(kept * factor)
        met = jnp.exp(met * factor)
        kept = jnp.concatenate([kept[:, :txt] * valid, kept[:, txt:]], axis=1)
        total = jnp.sum(lanes_summed(kept) + lanes_summed(met), axis=-1, keepdims=True)
        mixed = jnp.dot(
            kept.astype(BF16), values_kept[:, at], preferred_element_type=F32
        ) + jnp.dot(met.astype(BF16), values_met[:, at], preferred_element_type=F32)
        results.append(mixed / total)
    return jnp.concatenate(results, axis=1)


def relay_kernel(
    dims,
    block_hbm,
    fresh_hbm,
    w_hbm,
    shift_hbm,
    scale_hbm,
    gate_hbm,
    q_gain_hbm,
    k_gain_hbm,
    image_hbm,
    text_hbm,
    order_hbm,
    length_hbm,
    out_hbm,
    new_hbm,
    block,
    fresh,
    w,
    shift,
    scale,
    gate,
    q_gain,
    k_gain,
    image,
    text,
    order,
    length,
    plain_sum,
    shift_sum,
    keys_kept,
    values_kept,
    keys_met,
    values_met,
    new,
    stream,
    sent,
    row_send,
    row_recv,
    last_send,
    last_recv,
    out,
    load_sem,
    store_sem,
    row_send_sem,
    row_recv_sem,
    tick_send_sem,
    tick_recv_sem,
    last_send_sem,
    last_recv_sem,
):
    sections, group, ticks, patches, pr, width, local, hd, txt = dims
    heads = local // hd
    rows_dev = pr // group
    half = width // 2
    section = lax.axis_index("section")
    uly = lax.axis_index("uly")

    other = uly + 1 - 2 * lax.rem(uly, 2)
    across = [lax.rem(other + k, group) for k in (4, 2, 6, 0)]
    beside = [lax.rem(uly + k, group) for k in (4, 2, 6)]
    peers = across + beside
    nearest_first = [uly, *beside[1:], beside[0], across[3], across[1], across[2], across[0]]

    barrier = pltpu.get_barrier_semaphore()
    for p in peers:
        pl.semaphore_signal(barrier, inc=1, device_id=(section, p), device_id_type=MESH)

    @pl.when(section > 0)
    def _():
        for p in [*peers, uly]:
            pl.semaphore_signal(barrier, inc=1, device_id=(section - 1, p), device_id_type=MESH)

    loads = [
        pltpu.make_async_copy(src, dst, load_sem.at[i])
        for i, (src, dst) in enumerate(
            [
                (block_hbm, block),
                (fresh_hbm, fresh),
                (text_hbm, text),
                (k_gain_hbm, k_gain),
                (image_hbm, image),
                (order_hbm, order),
                (length_hbm, length),
                (shift_hbm, shift),
                (scale_hbm, scale),
                (gate_hbm, gate),
                (q_gain_hbm, q_gain),
                (w_hbm, w),
            ]
        )
    ]
    for copy in loads:
        copy.start()

    loads[0].wait()
    loads[1].wait()
    for t in range(ticks):
        own = block[...] if t == 0 else fresh[t - 1]
        own = own.astype(F32)
        own = jnp.concatenate([own[:, :half], own[:, half:]], axis=0).astype(BF16)
        row_send[t] = own
        row_recv[t, uly] = own

    for copy in loads[2:7]:
        copy.wait()
    k_row = k_gain[...]
    keys_kept[pl.ds(0, txt), :] = normed(text[0].astype(F32), k_row, hd).astype(BF16)
    values_kept[pl.ds(0, txt), :] = text[1]
    for j in range(patches):
        patch = order[lax.rem(j - section + sections * patches, patches)]
        met = []
        for i in range(2):
            rows = image[i, pl.ds(0, pr), :]
            for b in range(1, patches):
                rows = jnp.where(patch == b, image[i, pl.ds(b * pr, pr), :], rows)
            met.append(rows)
        keys, values, at = (
            (keys_met, values_met, pl.ds(j * pr, pr))
            if j < ticks
            else (keys_kept, values_kept, pl.ds(txt + (j - ticks) * pr, pr))
        )
        keys[at, :] = normed(met[0].astype(F32), k_row, hd).astype(BF16)
        values[at, :] = met[1]
    valid = (lax.broadcasted_iota(jnp.int32, (1, txt), 1) < length[0]).astype(F32)

    pl.semaphore_wait(barrier, group - 1 + jnp.where(section < sections - 1, group, 0))

    def row_copy(t, i):
        return pltpu.make_async_remote_copy(
            src_ref=row_send.at[t],
            dst_ref=row_recv.at[t, uly],
            send_sem=row_send_sem.at[t, i],
            recv_sem=row_recv_sem.at[t, uly],
            device_id=(section, peers[i]),
            device_id_type=MESH,
        )

    def row_arrival(t, p):
        return pltpu.make_async_remote_copy(
            src_ref=row_send.at[t],
            dst_ref=row_recv.at[t, p],
            send_sem=row_send_sem.at[t, 0],
            recv_sem=row_recv_sem.at[t, p],
            device_id=(section, p),
            device_id_type=MESH,
        )

    for i in range(group - 1):
        row_copy(0, i).start()

    @pl.when(section == 0)
    def _():
        for t in range(1, ticks):
            for i in range(group - 1):
                row_copy(t, i).start()

    for copy in loads[7:]:
        copy.wait()
    q_row = q_gain[...]
    fold(w, shift, scale, plain_sum, shift_sum, local)

    def rows_to_stream(t):
        for p in peers:
            row_arrival(t, p).wait_recv()
        pieces = [row_recv[t, i].astype(F32) for i in range(group)]
        for side in range(2):
            whole = jnp.concatenate(
                [piece[side * rows_dev : (side + 1) * rows_dev] for piece in pieces], axis=0
            ).astype(BF16)
            for c in range(group // 2):
                stream[t, side * (group // 2) + c] = whole[:, c * local : (c + 1) * local]

    def tick_copy(t, i, p):
        return pltpu.make_async_remote_copy(
            src_ref=sent.at[t],
            dst_ref=stream.at[t + 1, uly],
            send_sem=tick_send_sem.at[t, i],
            recv_sem=tick_recv_sem.at[t + 1, uly],
            device_id=(section + 1, p),
            device_id_type=MESH,
        )

    def tick_arrival(t, p):
        return pltpu.make_async_remote_copy(
            src_ref=sent.at[t],
            dst_ref=stream.at[t, p],
            send_sem=tick_send_sem.at[t, 0],
            recv_sem=tick_recv_sem.at[t, p],
            device_id=(section, uly),
            device_id_type=MESH,
        )

    def last_copy(i):
        return pltpu.make_async_remote_copy(
            src_ref=last_send.at[peers[i]],
            dst_ref=last_recv.at[uly],
            send_sem=last_send_sem.at[i],
            recv_sem=last_recv_sem.at[uly],
            device_id=(section, peers[i]),
            device_id_type=MESH,
        )

    def last_arrival(p):
        return pltpu.make_async_remote_copy(
            src_ref=last_send.at[p],
            dst_ref=last_recv.at[p],
            send_sem=last_send_sem.at[0],
            recv_sem=last_recv_sem.at[p],
            device_id=(section, p),
            device_id_type=MESH,
        )

    own_gate = gate[:, pl.ds(pl.multiple_of(uly * local, local), local)]
    for t in range(ticks):

        @pl.when(section == 0)
        def _():
            rows_to_stream(t)

        if t == 0:

            @pl.when(section > 0)
            def _():
                rows_to_stream(t)

        def arrived(c):
            if t > 0:

                @pl.when(section > 0)
                def _():
                    tick_arrival(t, c).wait_recv()

        queries, new_keys, new_values = project(
            stream.at[t], nearest_first, arrived, w, plain_sum, shift_sum, local, width
        )
        new_keys = new_keys.astype(BF16)
        new_values = new_values.astype(BF16)
        at = pl.ds(t * pr, pr)
        keys_met[at, :] = normed(new_keys.astype(F32), k_row, hd).astype(BF16)
        values_met[at, :] = new_values
        new[0, at, :] = new_keys
        new[1, at, :] = new_values
        attended = attend(
            queries, q_row, keys_kept, values_kept, keys_met, values_met, valid, hd
        )
        result = stream[t, uly].astype(F32) + own_gate * attended.astype(BF16).astype(F32)

        if t < ticks - 1:
            sent[t] = result.astype(BF16)

            @pl.when(section < sections - 1)
            def _():
                for i, p in enumerate([*peers, uly]):
                    tick_copy(t, i, p).start()
        else:
            for i in range(group):
                piece = result[i * rows_dev : (i + 1) * rows_dev]
                last_send[i] = jnp.concatenate(
                    [piece[:, c * hd : (c + 1) * hd] for c in range(heads)], axis=0
                ).astype(BF16)
            for i in range(group - 1):
                last_copy(i).start()
            last_recv[uly] = last_send[uly]

    store = pltpu.make_async_copy(new, new_hbm, store_sem.at[0])
    store.start()
    for i in range(group - 1):
        row_copy(0, i).wait_send()

    @pl.when(section == 0)
    def _():
        for t in range(1, ticks):
            for i in range(group - 1):
                row_copy(t, i).wait_send()

    @pl.when(section < sections - 1)
    def _():
        for t in range(ticks - 1):
            for i, p in enumerate([*peers, uly]):
                tick_copy(t, i, p).wait_send()

    for i in range(group - 1):
        last_copy(i).wait_send()
    store.wait()
    for p in peers:
        last_arrival(p).wait_recv()
    for i in range(group):
        piece = last_recv[i].astype(F32)
        for c in range(heads):
            out[:, pl.ds(i * local + c * hd, hd)] = piece[
                c * rows_dev : (c + 1) * rows_dev
            ].astype(BF16)
    store = pltpu.make_async_copy(out, out_hbm, store_sem.at[1])
    store.start()
    store.wait()


def store_kernel(dims, rows_hbm, new_hbm, image_hbm, order_hbm, out_hbm, cache_hbm, order, sems, order_sem):
    sections, _, ticks, patches, pr, *_ = dims
    section = lax.axis_index("section")
    load = pltpu.make_async_copy(order_hbm, order, order_sem)
    load.start()
    rows = pltpu.make_async_copy(rows_hbm, out_hbm, sems.at[2 * patches])
    rows.start()
    load.wait()
    met = [order[lax.rem(j - section + sections * patches, patches)] for j in range(ticks)]
    for b in range(patches):
        at = pl.ds(b * pr, pr)
        tick = jnp.int32(-1)
        for j in range(ticks):
            tick = jnp.where(met[j] == b, j, tick)

        @pl.when(tick >= 0)
        def _():
            start = pl.multiple_of(tick * pr, pr)
            for i in range(2):
                pltpu.make_async_copy(
                    new_hbm.at[i, pl.ds(start, pr), :], cache_hbm.at[i, at, :], sems.at[2 * b + i]
                ).start()

        @pl.when(tick < 0)
        def _():
            for i in range(2):
                pltpu.make_async_copy(
                    image_hbm.at[i, at, :], cache_hbm.at[i, at, :], sems.at[2 * b + i]
                ).start()

    rows.wait()
    for b in range(patches):
        at = pl.ds(b * pr, pr)
        for i in range(2):
            pltpu.make_async_copy(
                image_hbm.at[i, at, :], cache_hbm.at[i, at, :], sems.at[2 * b + i]
            ).wait()


def body(
    block_in,
    fresh_patches,
    w_qkv,
    mod_shift,
    mod_scale,
    gate,
    q_gain,
    k_gain,
    image_cache,
    text_cache,
    patch_order,
    text_length,
):
    sections, group = lax.axis_size("section"), lax.axis_size("uly")
    rows_dev, width = block_in.shape[1:]
    local = w_qkv.shape[3]
    hd = q_gain.shape[1]
    patches = patch_order.shape[0]
    ticks = fresh_patches.shape[0] + 1
    pr = rows_dev * group
    txt = text_cache.shape[2]
    img = patches * pr
    heads = local // hd
    kept = txt + (patches - ticks) * pr
    dims = (sections, group, ticks, patches, pr, width, local, hd, txt)
    hbm = pl.BlockSpec(memory_space=pl.ANY)
    dma = pltpu.SemaphoreType.DMA
    vmem = pltpu.VMEM
    rows, new = pl.pallas_call(
        functools.partial(relay_kernel, dims),
        out_shape=(
            jax.ShapeDtypeStruct((rows_dev, width), BF16),
            jax.ShapeDtypeStruct((2, ticks * pr, local), BF16),
        ),
        in_specs=[hbm] * 12,
        out_specs=(hbm, hbm),
        scratch_shapes=[
            vmem((rows_dev, width), BF16),
            vmem((ticks - 1, rows_dev, width), BF16),
            vmem((3, width, local), BF16),
            vmem((1, width), F32),
            vmem((1, width), F32),
            vmem((1, width), F32),
            vmem((1, hd), F32),
            vmem((1, hd), F32),
            vmem((2, img, local), BF16),
            vmem((2, txt, local), BF16),
            pltpu.SMEM((patches,), jnp.int32),
            pltpu.SMEM((1,), jnp.int32),
            vmem((3, 1, local), F32),
            vmem((3, 1, local), F32),
            vmem((kept, local), BF16),
            vmem((kept, local), BF16),
            vmem((ticks * pr, local), BF16),
            vmem((ticks * pr, local), BF16),
            vmem((2, ticks * pr, local), BF16),
            vmem((ticks, group, pr, local), BF16),
            vmem((ticks, pr, local), BF16),
            vmem((ticks, 2 * rows_dev, width // 2), BF16),
            vmem((ticks, group, 2 * rows_dev, width // 2), BF16),
            vmem((group, heads * rows_dev, hd), BF16),
            vmem((group, heads * rows_dev, hd), BF16),
            vmem((rows_dev, width), BF16),
            dma((12,)),
            dma((2,)),
            dma((ticks, group)),
            dma((ticks, group)),
            dma((ticks, group)),
            dma((ticks, group)),
            dma((group,)),
            dma((group,)),
        ],
        compiler_params=pltpu.CompilerParams(
            collective_id=0, has_side_effects=True, vmem_limit_bytes=VMEM_LIMIT
        ),
        name="relay",
    )(
        block_in[0],
        fresh_patches,
        jnp.transpose(w_qkv[0], (1, 0, 2)),
        mod_shift,
        mod_scale,
        gate,
        q_gain,
        k_gain,
        image_cache[0],
        text_cache[0],
        patch_order,
        text_length,
    )
    out, cache = pl.pallas_call(
        functools.partial(store_kernel, dims),
        out_shape=(
            jax.ShapeDtypeStruct((rows_dev, width), BF16),
            jax.ShapeDtypeStruct((2, img, local), BF16),
        ),
        in_specs=[hbm] * 4,
        out_specs=(hbm, hbm),
        scratch_shapes=[
            pltpu.SMEM((patches,), jnp.int32),
            dma((2 * patches + 1,)),
            dma,
        ],
        compiler_params=pltpu.CompilerParams(vmem_limit_bytes=VMEM_LIMIT),
        name="outputs",
    )(rows, new, image_cache[0], patch_order)
    return out[None], cache[None]


def solution(mesh):
    in_specs = (
        P("section", "uly", None),
        P(None, "uly", None),
        P("section", None, None, "uly"),
        P("section", None),
        P("section", None),
        P("section", None),
        P("section", None),
        P("section", None),
        P("section", None, None, "uly"),
        P("section", None, None, "uly"),
        P(),
        P(),
    )
    out_specs = (P("section", "uly", None), P("section", None, None, "uly"))
    return jax.shard_map(body, mesh=mesh, in_specs=in_specs, out_specs=out_specs, check_vma=False)
```

time: 70.7 us -> 81.8 us (1.16)
  Pallas kernels: 65.9 us -> 80.3 us
  local copies, waits for them, and re-layouts: 3.24 us -> 0 us
    pallas_call x1 -> x2, Pallas kernels: 65.9 us -> 80.3 us  [the longest x1 62.2 us: body(): pl.pallas_call(functools.partial(relay_kernel, dims), out_shape=(jax.Shap...]
    unnamed x2 -> x0, local copies, waits for them, and re-layouts: 3.24 us -> none
where the time goes in v2:
time: 81.8 us; the launch traced here: 81.6 us
  Pallas kernels  80.3 us (98%)
  between operations  1.29 us (2%)
    pallas_call x1, Pallas kernels, body(): pl.pallas_call(functools.partial(relay_kernel, dims), out_shape=(jax.Shap...  62.2 us
    pallas_call x1, Pallas kernels, body(): pl.pallas_call(functools.partial(store_kernel, dims), out_shape=(jax.Shap...  18.1 us

profile of v2, /device:TPU:16, one launch (start us, length us, event | category | flops | bytes accessed | tf_op | source)
XLA Modules:
  0.0 81.6 jit_solution(1099524650735746315)
XLA Ops:
  1.3 62.2 %relay.1 = (bf16[8,2048]{1,0:T(8,128)(2,1)}, bf16[2,256,256]{2,1,0:T(8,128)(2,1)}) custom-call(bf16[8,2048]{1,0:T(8,128)(2,1)} %bitcast.12, bf16[3,8,2048]{2,1,0:T(8,128)(2,1)} %fresh_hbm.1, bf16[3,2048,256]{2,1,0:T(8,128)(2,1)} %bitcast.8, f32[1,2048]{1,0:T(1,128)} %shift_hbm.1, f32[1,2048]{1,0:T(1,128)} %scale_hbm.1, f32[1,2048]{1,0:T(1,128)} %gate_hbm.1, ...), custom_call_target="tpu_custom_call" | custom-call | tf_op jit(solution)/shard_map/relay/pallas_call | solution.py:495
  63.5 18.1 %outputs.1 = (bf16[8,2048]{1,0:T(8,128)(2,1)}, bf16[2,512,256]{2,1,0:T(8,128)(2,1)}) custom-call(bf16[8,2048]{1,0:T(8,128)(2,1)} %get-tuple-element.6.rows_hbm, bf16[2,256,256]{2,1,0:T(8,128)(2,1)} %get-tuple-element.7.new_hbm, bf16[2,512,256]{2,1,0:T(8,128)(2,1)} %bitcast.10, s32[8]{0:T(128)} %order_hbm.3), custom_call_target="tpu_custom_call" | custom-call | tf_op jit(solution)/shard_map/outputs/pallas_call | solution.py:557

commit v3 on v2

--- a/solution.py
+++ b/solution.py
@@ -105,25 +105,31 @@
 
 
 def attend(queries, q_row, keys_kept, values_kept, keys_met, values_met, valid, hd):
-    txt = valid.shape[1]
-    results = []
-    for start in range(0, queries.shape[1], hd):
-        at = slice(start, start + hd)
-        query = queries[:, at]
-        factor = head_factor(query) * (1.0 / math.sqrt(hd))
-        query = (query * q_row).astype(BF16)
-        contract = (((1,), (1,)), ((), ()))
-        kept = lax.dot_general(query, keys_kept[:, at], contract, preferred_element_type=F32)
-        met = lax.dot_general(query, keys_met[:, at], contract, preferred_element_type=F32)
-        kept = jnp.exp(kept * factor)
-        met = jnp.exp(met * factor)
-        kept = jnp.concatenate([kept[:, :txt] * valid, kept[:, txt:]], axis=1)
-        total = jnp.sum(lanes_summed(kept) + lanes_summed(met), axis=-1, keepdims=True)
-        mixed = jnp.dot(
-            kept.astype(BF16), values_kept[:, at], preferred_element_type=F32
-        ) + jnp.dot(met.astype(BF16), values_met[:, at], preferred_element_type=F32)
-        results.append(mixed / total)
-    return jnp.concatenate(results, axis=1)
+    rows, txt = queries.shape[0], valid.shape[1]
+    heads = queries.shape[1] // hd
+    stacked, factors = [], []
+    for h in range(heads):
+        query = queries[:, h * hd : (h + 1) * hd]
+        factors.append(head_factor(query) * (1.0 / math.sqrt(hd)))
+        parts = [jnp.zeros((rows, hd), BF16)] * heads
+        parts[h] = (query * q_row).astype(BF16)
+        stacked.append(jnp.concatenate(parts, axis=1))
+    stacked = jnp.concatenate(stacked, axis=0)
+    factor = jnp.concatenate(factors, axis=0)
+    contract = (((1,), (1,)), ((), ()))
+    kept = lax.dot_general(stacked, keys_kept[...], contract, preferred_element_type=F32)
+    met = lax.dot_general(stacked, keys_met[...], contract, preferred_element_type=F32)
+    kept = jnp.exp(kept * factor)
+    met = jnp.exp(met * factor)
+    kept = jnp.concatenate([kept[:, :txt] * valid, kept[:, txt:]], axis=1)
+    total = jnp.sum(lanes_summed(kept) + lanes_summed(met), axis=-1, keepdims=True)
+    mixed = jnp.dot(
+        kept.astype(BF16), values_kept[...], preferred_element_type=F32
+    ) + jnp.dot(met.astype(BF16), values_met[...], preferred_element_type=F32)
+    mixed = mixed / total
+    return jnp.concatenate(
+        [mixed[h * rows : (h + 1) * rows, h * hd : (h + 1) * hd] for h in range(heads)], axis=1
+    )
 
 
 def relay_kernel(
@@ -424,43 +430,48 @@
     store.wait()
 
 
-def store_kernel(dims, rows_hbm, new_hbm, image_hbm, order_hbm, out_hbm, cache_hbm, order, sems, order_sem):
+def store_kernel(
+    dims, rows_hbm, new_hbm, image_hbm, order_hbm, out_hbm, cache_hbm, rows, new, cache, order, load_sem, store_sem
+):
     sections, _, ticks, patches, pr, *_ = dims
     section = lax.axis_index("section")
-    load = pltpu.make_async_copy(order_hbm, order, order_sem)
-    load.start()
-    rows = pltpu.make_async_copy(rows_hbm, out_hbm, sems.at[2 * patches])
-    rows.start()
-    load.wait()
+    loads = [
+        pltpu.make_async_copy(src, dst, load_sem.at[i])
+        for i, (src, dst) in enumerate(
+            [
+                (order_hbm, order),
+                (image_hbm.at[0], cache.at[0]),
+                (image_hbm.at[1], cache.at[1]),
+                (new_hbm, new),
+                (rows_hbm, rows),
+            ]
+        )
+    ]
+    for copy in loads:
+        copy.start()
+    stores = [
+        pltpu.make_async_copy(src, dst, store_sem.at[i])
+        for i, (src, dst) in enumerate(
+            [
+                (cache.at[0], cache_hbm.at[0]),
+                (cache.at[1], cache_hbm.at[1]),
+                (rows, out_hbm),
+            ]
+        )
+    ]
+    loads[4].wait()
+    stores[2].start()
+    loads[0].wait()
     met = [order[lax.rem(j - section + sections * patches, patches)] for j in range(ticks)]
-    for b in range(patches):
-        at = pl.ds(b * pr, pr)
-        tick = jnp.int32(-1)
+    loads[3].wait()
+    for i in range(2):
+        loads[1 + i].wait()
         for j in range(ticks):
-            tick = jnp.where(met[j] == b, j, tick)
-
-        @pl.when(tick >= 0)
-        def _():
-            start = pl.multiple_of(tick * pr, pr)
-            for i in range(2):
-                pltpu.make_async_copy(
-                    new_hbm.at[i, pl.ds(start, pr), :], cache_hbm.at[i, at, :], sems.at[2 * b + i]
-                ).start()
-
-        @pl.when(tick < 0)
-        def _():
-            for i in range(2):
-                pltpu.make_async_copy(
-                    image_hbm.at[i, at, :], cache_hbm.at[i, at, :], sems.at[2 * b + i]
-                ).start()
-
-    rows.wait()
-    for b in range(patches):
-        at = pl.ds(b * pr, pr)
-        for i in range(2):
-            pltpu.make_async_copy(
-                image_hbm.at[i, at, :], cache_hbm.at[i, at, :], sems.at[2 * b + i]
-            ).wait()
+            at = pl.ds(pl.multiple_of(met[j] * pr, pr), pr)
+            cache[i, at, :] = new[i, pl.ds(j * pr, pr), :]
+        stores[i].start()
+    for copy in stores:
+        copy.wait()
 
 
 def body(
@@ -563,9 +574,12 @@
         in_specs=[hbm] * 4,
         out_specs=(hbm, hbm),
         scratch_shapes=[
+            vmem((rows_dev, width), BF16),
+            vmem((2, ticks * pr, local), BF16),
+            vmem((2, img, local), BF16),
             pltpu.SMEM((patches,), jnp.int32),
-            dma((2 * patches + 1,)),
-            dma,
+            dma((5,)),
+            dma((3,)),
         ],
         compiler_params=pltpu.CompilerParams(vmem_limit_bytes=VMEM_LIMIT),
         name="outputs",

time: 81.8 us -> 64.9 us (0.79)
  Pallas kernels: 80.3 us -> 63.5 us
    pallas_call x1, Pallas kernels: 18.1 us -> 1.98 us  [body(): pl.pallas_call(functools.partial(store_kernel, dims), out_shape=(jax.Shap...]
where the time goes in v3:
time: 64.9 us; the launch traced here: 64.7 us
  Pallas kernels  63.5 us (98%)
  between operations  1.29 us (2%)
    pallas_call x1, Pallas kernels, body(): pl.pallas_call(functools.partial(relay_kernel, dims), out_shape=(jax.Shap...  61.5 us
    pallas_call x1, Pallas kernels, body(): pl.pallas_call(functools.partial(store_kernel, dims), out_shape=(jax.Shap...  1.98 us

profile of v3, /device:TPU:16, one launch (start us, length us, event | category | flops | bytes accessed | tf_op | source)
XLA Modules:
  0.0 64.7 jit_solution(13999906553553850091)
XLA Ops:
  1.3 61.5 %relay.1 = (bf16[8,2048]{1,0:T(8,128)(2,1)}, bf16[2,256,256]{2,1,0:T(8,128)(2,1)}) custom-call(bf16[8,2048]{1,0:T(8,128)(2,1)} %bitcast.12, bf16[3,8,2048]{2,1,0:T(8,128)(2,1)} %fresh_hbm.1, bf16[3,2048,256]{2,1,0:T(8,128)(2,1)} %bitcast.8, f32[1,2048]{1,0:T(1,128)} %shift_hbm.1, f32[1,2048]{1,0:T(1,128)} %scale_hbm.1, f32[1,2048]{1,0:T(1,128)} %gate_hbm.1, ...), custom_call_target="tpu_custom_call" | custom-call | tf_op jit(solution)/shard_map/relay/pallas_call | solution.py:506
  62.8 2.0 %outputs.1 = (bf16[8,2048]{1,0:T(8,128)(2,1)}, bf16[2,512,256]{2,1,0:T(8,128)(2,1)}) custom-call(bf16[8,2048]{1,0:T(8,128)(2,1)} %get-tuple-element.6.rows_hbm, bf16[2,256,256]{2,1,0:T(8,128)(2,1)} %get-tuple-element.7.new_hbm, bf16[2,512,256]{2,1,0:T(8,128)(2,1)} %bitcast.10, s32[8]{0:T(128)} %order_hbm.3), custom_call_target="tpu_custom_call" | custom-call | tf_op jit(solution)/shard_map/outputs/pallas_call | solution.py:568

commit v4 on v3

--- a/solution.py
+++ b/solution.py
@@ -12,7 +12,7 @@
 F32 = jnp.float32
 BF16 = jnp.bfloat16
 EPS = 1e-06
-VMEM_LIMIT = 63 * 1024 * 1024
+VMEM_LIMIT = 48 * 1024 * 1024
 
 
 def head_factor(values):
@@ -146,8 +146,8 @@
     text_hbm,
     order_hbm,
     length_hbm,
-    out_hbm,
-    new_hbm,
+    out,
+    cache_out,
     block,
     fresh,
     w,
@@ -173,9 +173,7 @@
     row_recv,
     last_send,
     last_recv,
-    out,
     load_sem,
-    store_sem,
     row_send_sem,
     row_recv_sem,
     tick_send_sem,
@@ -193,7 +191,7 @@
     other = uly + 1 - 2 * lax.rem(uly, 2)
     across = [lax.rem(other + k, group) for k in (4, 2, 6, 0)]
     beside = [lax.rem(uly + k, group) for k in (4, 2, 6)]
-    peers = across + beside
+    peers = [across[0], beside[0], across[1], beside[1], across[2], beside[2], across[3]]
     nearest_first = [uly, *beside[1:], beside[0], across[3], across[1], across[2], across[0]]
 
     barrier = pltpu.get_barrier_semaphore()
@@ -236,13 +234,16 @@
         row_send[t] = own
         row_recv[t, uly] = own
 
+    def patch_at(slot):
+        return order[lax.rem(slot - section + sections * patches, patches)]
+
     for copy in loads[2:7]:
         copy.wait()
     k_row = k_gain[...]
     keys_kept[pl.ds(0, txt), :] = normed(text[0].astype(F32), k_row, hd).astype(BF16)
     values_kept[pl.ds(0, txt), :] = text[1]
     for j in range(patches):
-        patch = order[lax.rem(j - section + sections * patches, patches)]
+        patch = patch_at(j)
         met = []
         for i in range(2):
             rows = image[i, pl.ds(0, pr), :]
@@ -280,6 +281,15 @@
             device_id_type=MESH,
         )
 
+    for copy in loads[7:]:
+        copy.wait()
+    q_row = q_gain[...]
+    even = lax.rem(section, 2) == 0
+
+    @pl.when(even)
+    def _():
+        fold(w, shift, scale, plain_sum, shift_sum, local)
+
     for i in range(group - 1):
         row_copy(0, i).start()
 
@@ -289,10 +299,9 @@
             for i in range(group - 1):
                 row_copy(t, i).start()
 
-    for copy in loads[7:]:
-        copy.wait()
-    q_row = q_gain[...]
-    fold(w, shift, scale, plain_sum, shift_sum, local)
+    @pl.when(jnp.logical_not(even))
+    def _():
+        fold(w, shift, scale, plain_sum, shift_sum, local)
 
     def rows_to_stream(t):
         for p in peers:
@@ -397,8 +406,12 @@
                 last_copy(i).start()
             last_recv[uly] = last_send[uly]
 
-    store = pltpu.make_async_copy(new, new_hbm, store_sem.at[0])
-    store.start()
+    for b in range(patches):
+        for i in range(2):
+            rows = image[i, pl.ds(b * pr, pr), :]
+            for j in range(ticks):
+                rows = jnp.where(patch_at(j) == b, new[i, pl.ds(j * pr, pr), :], rows)
+            cache_out[i, pl.ds(b * pr, pr), :] = rows
     for i in range(group - 1):
         row_copy(0, i).wait_send()
 
@@ -416,7 +429,6 @@
 
     for i in range(group - 1):
         last_copy(i).wait_send()
-    store.wait()
     for p in peers:
         last_arrival(p).wait_recv()
     for i in range(group):
@@ -425,53 +437,25 @@
             out[:, pl.ds(i * local + c * hd, hd)] = piece[
                 c * rows_dev : (c + 1) * rows_dev
             ].astype(BF16)
-    store = pltpu.make_async_copy(out, out_hbm, store_sem.at[1])
-    store.start()
-    store.wait()
-
-
-def store_kernel(
-    dims, rows_hbm, new_hbm, image_hbm, order_hbm, out_hbm, cache_hbm, rows, new, cache, order, load_sem, store_sem
-):
-    sections, _, ticks, patches, pr, *_ = dims
-    section = lax.axis_index("section")
-    loads = [
-        pltpu.make_async_copy(src, dst, load_sem.at[i])
-        for i, (src, dst) in enumerate(
-            [
-                (order_hbm, order),
-                (image_hbm.at[0], cache.at[0]),
-                (image_hbm.at[1], cache.at[1]),
-                (new_hbm, new),
-                (rows_hbm, rows),
-            ]
-        )
+
+
+def store_kernel(rows, cache, out_hbm, cache_hbm, sems):
+    copies = [
+        pltpu.make_async_copy(src, dst, sems.at[i])
+        for i, (src, dst) in enumerate([(rows, out_hbm), (cache, cache_hbm)])
     ]
-    for copy in loads:
+    for copy in copies:
         copy.start()
-    stores = [
-        pltpu.make_async_copy(src, dst, store_sem.at[i])
-        for i, (src, dst) in enumerate(
-            [
-                (cache.at[0], cache_hbm.at[0]),
-                (cache.at[1], cache_hbm.at[1]),
-                (rows, out_hbm),
-            ]
-        )
-    ]
-    loads[4].wait()
-    stores[2].start()
-    loads[0].wait()
-    met = [order[lax.rem(j - section + sections * patches, patches)] for j in range(ticks)]
-    loads[3].wait()
-    for i in range(2):
-        loads[1 + i].wait()
-        for j in range(ticks):
-            at = pl.ds(pl.multiple_of(met[j] * pr, pr), pr)
-            cache[i, at, :] = new[i, pl.ds(j * pr, pr), :]
-        stores[i].start()
-    for copy in stores:
+    for copy in copies:
         copy.wait()
+
+
+def in_hbm(*arrays):
+    return [pltpu.with_memory_space_constraint(array, pltpu.HBM) for array in arrays]
+
+
+def in_vmem(*arrays):
+    return [pltpu.with_memory_space_constraint(array, pltpu.VMEM) for array in arrays]
 
 
 def body(
@@ -503,14 +487,14 @@
     hbm = pl.BlockSpec(memory_space=pl.ANY)
     dma = pltpu.SemaphoreType.DMA
     vmem = pltpu.VMEM
-    rows, new = pl.pallas_call(
+    rows, cache = pl.pallas_call(
         functools.partial(relay_kernel, dims),
         out_shape=(
             jax.ShapeDtypeStruct((rows_dev, width), BF16),
-            jax.ShapeDtypeStruct((2, ticks * pr, local), BF16),
+            jax.ShapeDtypeStruct((2, img, local), BF16),
         ),
         in_specs=[hbm] * 12,
-        out_specs=(hbm, hbm),
+        out_specs=(pl.BlockSpec(memory_space=pltpu.VMEM),) * 2,
         scratch_shapes=[
             vmem((rows_dev, width), BF16),
             vmem((ticks - 1, rows_dev, width), BF16),
@@ -537,9 +521,7 @@
             vmem((ticks, group, 2 * rows_dev, width // 2), BF16),
             vmem((group, heads * rows_dev, hd), BF16),
             vmem((group, heads * rows_dev, hd), BF16),
-            vmem((rows_dev, width), BF16),
             dma((12,)),
-            dma((2,)),
             dma((ticks, group)),
             dma((ticks, group)),
             dma((ticks, group)),
@@ -552,38 +534,33 @@
         ),
         name="relay",
     )(
-        block_in[0],
-        fresh_patches,
-        jnp.transpose(w_qkv[0], (1, 0, 2)),
-        mod_shift,
-        mod_scale,
-        gate,
-        q_gain,
-        k_gain,
-        image_cache[0],
-        text_cache[0],
-        patch_order,
+        *in_hbm(
+            block_in[0],
+            fresh_patches,
+            jnp.transpose(w_qkv[0], (1, 0, 2)),
+            mod_shift,
+            mod_scale,
+            gate,
+            q_gain,
+            k_gain,
+            image_cache[0],
+            text_cache[0],
+            patch_order,
+        ),
         text_length,
     )
     out, cache = pl.pallas_call(
-        functools.partial(store_kernel, dims),
+        store_kernel,
         out_shape=(
             jax.ShapeDtypeStruct((rows_dev, width), BF16),
             jax.ShapeDtypeStruct((2, img, local), BF16),
         ),
-        in_specs=[hbm] * 4,
+        in_specs=[hbm] * 2,
         out_specs=(hbm, hbm),
-        scratch_shapes=[
-            vmem((rows_dev, width), BF16),
-            vmem((2, ticks * pr, local), BF16),
-            vmem((2, img, local), BF16),
-            pltpu.SMEM((patches,), jnp.int32),
-            dma((5,)),
-            dma((3,)),
-        ],
+        scratch_shapes=[dma((2,))],
         compiler_params=pltpu.CompilerParams(vmem_limit_bytes=VMEM_LIMIT),
         name="outputs",
-    )(rows, new, image_cache[0], patch_order)
+    )(*in_vmem(rows, cache))
     return out[None], cache[None]
 
 

time: 64.9 us -> 61.3 us (0.945)
  the two profiles are of different devices: /device:TPU:16 before, /device:TPU:8 now
where the time goes in v4:
time: 61.3 us; the launch traced here: 61.2 us
  Pallas kernels  59.9 us (98%)
  between operations  1.29 us (2%)
    pallas_call x1, Pallas kernels, body(): pl.pallas_call(functools.partial(relay_kernel, dims), out_shape=(jax.Shap...  59.1 us

profile of v4, /device:TPU:8, one launch (start us, length us, event | category | flops | bytes accessed | tf_op | source)
XLA Modules:
  0.0 61.2 jit_solution(6322478652667838770)
XLA Ops:
  1.3 59.1 %relay.1 = (bf16[8,2048]{1,0:T(8,128)(2,1)S(1)}, bf16[2,512,256]{2,1,0:T(8,128)(2,1)S(1)}) custom-call(bf16[8,2048]{1,0:T(8,128)(2,1)} %bitcast.11, bf16[3,8,2048]{2,1,0:T(8,128)(2,1)} %fresh_hbm.1, bf16[3,2048,256]{2,1,0:T(8,128)(2,1)} %bitcast.8, f32[1,2048]{1,0:T(1,128)} %shift_hbm.1, f32[1,2048]{1,0:T(1,128)} %scale_hbm.1, f32[1,2048]{1,0:T(1,128)} %gate_hbm.1, ...), custom_call_target="tpu_custom_call" | custom-call | tf_op jit(solution)/shard_map/relay/pallas_call | solution.py:490
  60.3 0.8 %outputs.1 = (bf16[8,2048]{1,0:T(8,128)(2,1)}, bf16[2,512,256]{2,1,0:T(8,128)(2,1)}) custom-call(bf16[8,2048]{1,0:T(8,128)(2,1)S(1)} %get-tuple-element.6.rows, bf16[2,512,256]{2,1,0:T(8,128)(2,1)S(1)} %get-tuple-element.7.cache), custom_call_target="tpu_custom_call" | custom-call | tf_op jit(solution)/shard_map/outputs/pallas_call | solution.py:552

commit v5 on v4

--- a/solution.py
+++ b/solution.py
@@ -27,8 +27,7 @@
     return jnp.concatenate(parts, axis=1)
 
 
-def fold(w, shift, scale, plain_sum, shift_sum, local):
-    width = w.shape[1]
+def fold(w, shift, scale, plain_sum, shift_sum, local, start, stop):
     block = 256
     first = lax.broadcasted_iota(jnp.int32, (16, block), 0)
     ones = jnp.ones((16, block), BF16)
@@ -60,10 +59,10 @@
         return tuple(new)
 
     zero = jnp.zeros((16, local), F32)
-    totals = lax.fori_loop(0, width // block, step, (zero,) * 6)
+    totals = lax.fori_loop(start, stop, step, (zero,) * 6)
     for j in range(3):
-        plain_sum[j] = totals[2 * j][:1]
-        shift_sum[j] = totals[2 * j + 1][:1] + totals[2 * j + 1][1:2]
+        plain_sum[j] += totals[2 * j][:1]
+        shift_sum[j] += totals[2 * j + 1][:1] + totals[2 * j + 1][1:2]
 
 
 def lanes_summed(values):
@@ -191,7 +190,7 @@
     other = uly + 1 - 2 * lax.rem(uly, 2)
     across = [lax.rem(other + k, group) for k in (4, 2, 6, 0)]
     beside = [lax.rem(uly + k, group) for k in (4, 2, 6)]
-    peers = [across[0], beside[0], across[1], beside[1], across[2], beside[2], across[3]]
+    peers = across + beside
     nearest_first = [uly, *beside[1:], beside[0], across[3], across[1], across[2], across[0]]
 
     barrier = pltpu.get_barrier_semaphore()
@@ -284,11 +283,11 @@
     for copy in loads[7:]:
         copy.wait()
     q_row = q_gain[...]
-    even = lax.rem(section, 2) == 0
-
-    @pl.when(even)
-    def _():
-        fold(w, shift, scale, plain_sum, shift_sum, local)
+    plain_sum[...] = jnp.zeros_like(plain_sum)
+    shift_sum[...] = jnp.zeros_like(shift_sum)
+    blocks = width // 256
+    ahead = jnp.where(lax.rem(section, 2) == 0, blocks * 3 // 4, 0)
+    fold(w, shift, scale, plain_sum, shift_sum, local, 0, ahead)
 
     for i in range(group - 1):
         row_copy(0, i).start()
@@ -299,9 +298,7 @@
             for i in range(group - 1):
                 row_copy(t, i).start()
 
-    @pl.when(jnp.logical_not(even))
-    def _():
-        fold(w, shift, scale, plain_sum, shift_sum, local)
+    fold(w, shift, scale, plain_sum, shift_sum, local, ahead, blocks)
 
     def rows_to_stream(t):
         for p in peers:

time: 61.3 us -> 60.1 us (0.980)
  the two profiles are of different devices: /device:TPU:8 before, /device:TPU:9 now
where the time goes in v5:
time: 60.1 us; the launch traced here: 59.9 us
  Pallas kernels  58.7 us (98%)
  between operations  1.29 us (2%)
    pallas_call x1, Pallas kernels, body(): pl.pallas_call(functools.partial(relay_kernel, dims), out_shape=(jax.Shap...  57.8 us

profile of v5, /device:TPU:9, one launch (start us, length us, event | category | flops | bytes accessed | tf_op | source)
XLA Modules:
  0.0 59.9 jit_solution(7117470198854880952)
XLA Ops:
  1.3 57.8 %relay.1 = (bf16[8,2048]{1,0:T(8,128)(2,1)S(1)}, bf16[2,512,256]{2,1,0:T(8,128)(2,1)S(1)}) custom-call(bf16[8,2048]{1,0:T(8,128)(2,1)} %bitcast.11, bf16[3,8,2048]{2,1,0:T(8,128)(2,1)} %fresh_hbm.1, bf16[3,2048,256]{2,1,0:T(8,128)(2,1)} %bitcast.8, f32[1,2048]{1,0:T(1,128)} %shift_hbm.1, f32[1,2048]{1,0:T(1,128)} %scale_hbm.1, f32[1,2048]{1,0:T(1,128)} %gate_hbm.1, ...), custom_call_target="tpu_custom_call" | custom-call | tf_op jit(solution)/shard_map/relay/pallas_call | solution.py:487
  59.1 0.8 %outputs.1 = (bf16[8,2048]{1,0:T(8,128)(2,1)}, bf16[2,512,256]{2,1,0:T(8,128)(2,1)}) custom-call(bf16[8,2048]{1,0:T(8,128)(2,1)S(1)} %get-tuple-element.6.rows, bf16[2,512,256]{2,1,0:T(8,128)(2,1)S(1)} %get-tuple-element.7.cache), custom_call_target="tpu_custom_call" | custom-call | tf_op jit(solution)/shard_map/outputs/pallas_call | solution.py:549
